TPU v7x, 512 devices: a whole 4x8x8 slice. The times are simulated.
512 devices in a mesh: row: 16 (over y, core), col: 8 (over z), layer: 4 (over x).
Axes of the slice: x: 4, y: 8, z: 8, core: 2. Of those that a mesh axis runs over, the one named last changes fastest.
Arguments:
- matrix: bfloat16 [131072, 512], P(('row', 'col')), may hold values from -1.5 to 1.5
- pattern: int32 [2048, 8], replicated, may hold values from 0 to 2047, as said below
Outputs:
- sign_matrix: bfloat16 [131072, 512], P(('row', 'col'))
Inputs may be any that keep to these rules, and one draw needn't show every extreme that they name: `pattern`: row i lists 8 different block columns; its first entry is i, and the others lie within 4 of i, counted cyclically modulo 2048.
All inputs are finite; a program needn't handle non-finite values.
Results may differ from a plain program's by a relative error of at most 0.0062.
Values may be sent and summed in bfloat16 or wider, within the bound.
A program may use at most 64 MiB of HBM per device.

v0:
```python
import jax
import jax.numpy as jnp
from jax import lax
from jax.sharding import PartitionSpec as P

BS = 64
W = 4
ITERS = 2


def from_behind(value, axis, steps):
    count = lax.axis_size(axis)
    pairs = [(source, (source + steps) % count) for source in range(count)]
    return lax.ppermute(value, axis, pairs)


def on_device(matrix, pattern):
    local_height, local_width = matrix.shape
    slot_count = local_width // BS
    block_rows = local_height // BS
    group_rows = 2
    group_count = block_rows // group_rows
    layer_count = lax.axis_size("layer")
    layer_index = lax.axis_index("layer")
    share_width = slot_count // layer_count
    total_blocks = pattern.shape[0]
    first_block = lax.axis_index(("row", "col")) * block_rows
    own_blocks = first_block + jnp.arange(block_rows, dtype=jnp.int32)
    own_pattern = lax.dynamic_slice_in_dim(pattern, first_block, block_rows, 0)
    offsets = (own_pattern - own_blocks[:, None] + W) % total_blocks - W
    extended_rows = jnp.arange(block_rows, dtype=jnp.int32)[:, None] + offsets + W
    neighbour = jnp.take(pattern, own_pattern, axis=0)
    matches = neighbour[:, :, None, :] == own_pattern[:, None, :, None]
    present = jnp.any(matches, axis=3)
    slot_numbers = jnp.arange(slot_count, dtype=jnp.int32)
    picked_slot = jnp.sum(jnp.where(matches, slot_numbers, 0), axis=3)
    selector = jnp.where(
        (picked_slot[:, :, :, None] == slot_numbers) & present[:, :, :, None], 1.0, 0.0
    ).astype(jnp.bfloat16)
    row_groups = extended_rows.reshape(group_count, group_rows, slot_count)
    row_number = jnp.arange(local_height, dtype=jnp.int32)[:, None]
    column_number = jnp.arange(local_width, dtype=jnp.int32)[None, :]
    identity = jnp.where(
        (column_number < BS) & (column_number == row_number % BS), 1.0, 0.0
    ).astype(jnp.float32)

    def extend_rows(tile):
        rim_height = W * BS
        lower_rim = tile[:rim_height]
        upper_rim = tile[local_height - rim_height :]
        from_before = from_behind(upper_rim, ("row", "col"), 1)
        from_after = from_behind(lower_rim, ("row", "col"), -1)
        stacked = jnp.concatenate([from_before, tile, from_after], axis=0)
        return stacked.reshape(block_rows + 2 * W, BS, local_width)

    def masked_product(left, extended, start, count):
        left_groups = left.reshape(group_count, group_rows, BS, slot_count, BS)
        chosen_selector = lax.dynamic_slice_in_dim(selector, start, count, 2)
        selector_groups = chosen_selector.reshape(
            group_count, group_rows, slot_count, count, slot_count
        )

        def one_group(inputs):
            left_part, index_part, select_part = inputs
            gathered = jnp.take(extended, index_part, axis=0)
            gathered = gathered.reshape(group_rows, slot_count, BS, slot_count, BS)
            arranged = jnp.einsum(
                "rsbtc,rszt->rsbzc", gathered, select_part, preferred_element_type=jnp.float32
            ).astype(jnp.bfloat16)
            arranged = arranged.reshape(group_rows, slot_count, BS, count * BS)
            return jnp.einsum(
                "rasb,rsbx->rax", left_part, arranged, preferred_element_type=jnp.float32
            )

        total = lax.map(one_group, (left_groups, row_groups, selector_groups))
        return total.reshape(local_height, count * BS)

    current = matrix
    for iteration in range(ITERS):
        extended = extend_rows(current)
        square_part = masked_product(current, extended, layer_index * share_width, share_width)
        identity_part = lax.dynamic_slice_in_dim(
            identity, layer_index * share_width * BS, share_width * BS, 1
        )
        factor_part = (1.5 * identity_part - 0.5 * square_part).astype(jnp.bfloat16)
        factor = lax.all_gather(factor_part, "layer", axis=1, tiled=True)
        factor_extended = extend_rows(factor)
        renewed = masked_product(
            current, factor_extended, layer_index * share_width, share_width
        ).astype(jnp.bfloat16)
        current = lax.all_gather(renewed, "layer", axis=1, tiled=True)
    return current


def solution(mesh):
    return jax.shard_map(
        on_device,
        mesh=mesh,
        in_specs=(P(("row", "col"), None), P()),
        out_specs=P(("row", "col"), None),
        check_vma=False,
    )
```

profile of v0, /device:TPU:1, one launch (start us, length us, event | category | flops | bytes accessed | tf_op | source)
XLA Modules:
  0.0 412.5 jit_solution(7446203262755634418)
XLA Ops:
  6.5 1.9 fusion.47
  8.5 4.8 %collective-permute-start = (bf16[256,512]{1,0:T(8,128)(2,1)}, bf16[256,512]{1,0:T(8,128)(2,1)S(1)}, u32[]{:S(2)}, u32[]{:S(2)}) collective-permute-start(bf16[256,512]{1,0:T(8,128)(2,1)} %get-tuple-element.250), channel_id=1, source_target_pairs={{0,4},{4,8},{8,12},{12,16},{16,20},{20,24},{24,28},{28,32},{32,36}... | collective-permute-start | bytes 786440 | tf_op jit(solution)/shard_map/ppermute | solution.py:14
  13.3 9.1 %collective-permute-start.1 = (bf16[256,512]{1,0:T(8,128)(2,1)}, bf16[256,512]{1,0:T(8,128)(2,1)}, u32[]{:S(2)}, u32[]{:S(2)}) collective-permute-start(bf16[256,512]{1,0:T(8,128)(2,1)} %get-tuple-element.251), channel_id=1, source_target_pairs={{0,508},{4,0},{8,4},{12,8},{16,12},{20,16},{24,20},{28,24},{32,28}... | collective-permute-start | bytes 786440 | tf_op jit(solution)/shard_map/ppermute | solution.py:14
  27.1 1.9 copy.18
  30.2 2.2 pad_maximum_fusion
  33.2 49.5 %while.40 = (s32[]{:T(128)}, f32[8,2,64,128]{3,2,1,0:T(8,128)}, bf16[8,2,64,8,64]{4,2,3,1,0:T(8,128)(2,1)}, bf16[8,2,8,2,8]{4,3,2,1,0:T(2,128)(2,1)S(1)}, s32[8,...) while((s32[]{:T(128)}, f32[8,2,64,128]{3,2,1,0:T(8,128)}, ...), condition=%wide.region_3.5_spmd, body=%wide.region_2.4_spmd.sunk | while | flops 19530848 | bytes 9778677 | solution.py:75
  33.3 2.0 gather_fusion
  39.5 2.0 gather_fusion
  43.7 1.8 fusion.86
  45.7 2.0 gather_fusion
  51.9 2.0 gather_fusion
  56.1 1.8 fusion.86
  58.0 2.0 gather_fusion
  62.3 1.8 fusion.86
  64.2 2.0 gather_fusion
  68.5 1.8 fusion.86
  70.4 2.0 gather_fusion
  74.7 1.8 fusion.86
  76.6 2.0 gather_fusion
  80.9 1.8 fusion.86
  84.8 28.9 %all-gather.5.cloned.1.call-done = bf16[1024,512]{1,0:T(8,128)(2,1)} async-done(((bf16[1024,128]{1,0:T(8,128)(2,1)}), bf16[1024,512]{1,0:T(8,128)(2,1)}) %all-gather.5.cloned.1.call-update) | async-done | bytes 1048592 | tf_op jit(solution)/shard_map/all_gather | solution.py:86
  114.9 3.3 collective-permute-start.2
  118.1 5.7 %collective-permute-start.3 = (bf16[256,512]{1,0:T(8,128)(2,1)S(1)}, bf16[256,512]{1,0:T(8,128)(2,1)S(1)}, u32[]{:S(2)}, u32[]{:S(2)}) collective-permute-start(bf16[256,512]{1,0:T(8,128)(2,1)S(1)} %get-tuple-element.249), channel_id=1, source_target_pairs={{0,508},{4,0},{8,4},{12,8},{16,12},{20,16},{24,20},{28,24},{32,28}... | collective-permute-start | bytes 786440 | tf_op jit(solution)/shard_map/ppermute | solution.py:14
  124.6 4.2 %collective-permute-done.2 = bf16[256,512]{1,0:T(8,128)(2,1)S(1)} collective-permute-done((bf16[256,512]{1,0:T(8,128)(2,1)S(1)}, bf16[256,512]{1,0:T(8,128)(2,1)S(1)}, u32[]{:S(2)}, u32[]{:S(2)}) %collective-permute-start.2) | collective-permute-done | bytes 262176 | tf_op jit(solution)/shard_map/ppermute | solution.py:14
  131.1 49.4 %while.41 = (s32[]{:T(128)}, bf16[8,2,64,128]{3,2,1,0:T(8,128)(2,1)}, bf16[8,2,64,8,64]{4,2,3,1,0:T(8,128)(2,1)}, bf16[8,2,8,2,8]{4,3,2,1,0:T(2,128)(2,1)S(1)}, ...) while((s32[]{:T(128)}, bf16[8,2,64,128]{3,2,1,0:T(8,128)(2,1)}, ...), condition=%wide.region_5.7_spmd, body=%wide.region_4.6_spmd.sunk | while | flops 19530848 | bytes 9778677 | solution.py:75
  131.2 2.0 gather_fusion.1
  137.4 2.0 gather_fusion.1
  143.6 2.0 gather_fusion.1
  149.8 2.0 gather_fusion.1
  155.9 2.0 gather_fusion.1
  162.1 2.0 gather_fusion.1
  168.3 2.0 gather_fusion.1
  174.4 2.0 gather_fusion.1
  180.6 29.8 %all-gather.7.cloned.1.call-done = bf16[1024,512]{1,0:T(8,128)(2,1)} async-done(((bf16[1024,128]{1,0:T(8,128)(2,1)}), bf16[1024,512]{1,0:T(8,128)(2,1)}) %all-gather.7.cloned.1.call-update) | async-done | bytes 1048592 | tf_op jit(solution)/shard_map/all_gather | solution.py:91
  211.4 3.3 collective-permute-start.4
  214.7 5.7 %collective-permute-start.5 = (bf16[256,512]{1,0:T(8,128)(2,1)S(1)}, bf16[256,512]{1,0:T(8,128)(2,1)S(1)}, u32[]{:S(2)}, u32[]{:S(2)}) collective-permute-start(bf16[256,512]{1,0:T(8,128)(2,1)S(1)} %get-tuple-element.247), channel_id=1, source_target_pairs={{0,508},{4,0},{8,4},{12,8},{16,12},{20,16},{24,20},{28,24},{32,28}... | collective-permute-start | bytes 786440 | tf_op jit(solution)/shard_map/ppermute | solution.py:14
  220.4 2.8 reshape.108
  223.2 1.9 copy.20
  228.6 49.5 %while.42 = (s32[]{:T(128)}, f32[8,2,64,128]{3,2,1,0:T(8,128)}, bf16[8,2,64,8,64]{4,2,3,1,0:T(8,128)(2,1)}, bf16[8,2,8,2,8]{4,3,2,1,0:T(2,128)(2,1)S(1)}, s32[8,...) while((s32[]{:T(128)}, f32[8,2,64,128]{3,2,1,0:T(8,128)}, ...), condition=%wide.region_7.9_spmd, body=%wide.region_6.8_spmd.sunk | while | flops 19530848 | bytes 9778677 | solution.py:75
  228.7 2.0 gather_fusion.2
  232.9 1.8 fusion.98
  234.8 2.0 gather_fusion.2
  241.0 2.0 gather_fusion.2
  247.2 2.0 gather_fusion.2
  253.4 2.0 gather_fusion.2
  259.6 2.0 gather_fusion.2
  265.8 2.0 gather_fusion.2
  271.9 2.0 gather_fusion.2
  280.1 29.8 %all-gather.9.cloned.1.call-done = bf16[1024,512]{1,0:T(8,128)(2,1)} async-done(((bf16[1024,128]{1,0:T(8,128)(2,1)}), bf16[1024,512]{1,0:T(8,128)(2,1)}) %all-gather.9.cloned.1.call-update) | async-done | bytes 1048592 | tf_op jit(solution)/shard_map/all_gather | solution.py:86
  310.9 3.3 collective-permute-start.6
  314.2 5.7 %collective-permute-start.7 = (bf16[256,512]{1,0:T(8,128)(2,1)S(1)}, bf16[256,512]{1,0:T(8,128)(2,1)S(1)}, u32[]{:S(2)}, u32[]{:S(2)}) collective-permute-start(bf16[256,512]{1,0:T(8,128)(2,1)S(1)} %get-tuple-element.245), channel_id=1, source_target_pairs={{0,508},{4,0},{8,4},{12,8},{16,12},{20,16},{24,20},{28,24},{32,28}... | collective-permute-start | bytes 786440 | tf_op jit(solution)/shard_map/ppermute | solution.py:14
  319.9 4.9 %collective-permute-done.6 = bf16[256,512]{1,0:T(8,128)(2,1)S(1)} collective-permute-done((bf16[256,512]{1,0:T(8,128)(2,1)S(1)}, bf16[256,512]{1,0:T(8,128)(2,1)S(1)}, u32[]{:S(2)}, u32[]{:S(2)}) %collective-permute-start.6) | collective-permute-done | bytes 262176 | tf_op jit(solution)/shard_map/ppermute | solution.py:14
  326.0 2.5 pad_maximum_fusion.3
  328.5 44.7 %while.43 = (s32[]{:T(128)}, bf16[8,2,64,128]{3,2,1,0:T(8,128)(2,1)S(1)}, bf16[8,2,64,8,64]{4,2,3,1,0:T(8,128)(2,1)}, bf16[8,2,8,2,8]{4,3,2,1,0:T(2,128)(2,1)S(1...) while((s32[]{:T(128)}, bf16[8,2,64,128]{3,2,1,0:T(8,128)(2,1)S(1)}, ...), condition=%wide.region_9.11_spmd, body=%wide.region_8.10_spmd.sunk | while | flops 19530848 | bytes 9778677 | solution.py:75
  328.6 2.0 gather_fusion.3
  334.1 2.0 gather_fusion.3
  339.7 2.0 gather_fusion.3
  345.3 2.0 gather_fusion.3
  350.9 2.0 gather_fusion.3
  356.5 2.0 gather_fusion.3
  362.1 2.0 gather_fusion.3
  367.7 2.0 gather_fusion.3
  373.9 29.8 %all-gather.11.cloned.1.call-done = bf16[1024,512]{1,0:T(8,128)(2,1)} async-done(((bf16[1024,128]{1,0:T(8,128)(2,1)}), bf16[1024,512]{1,0:T(8,128)(2,1)}) %all-gather.11.cloned.1.call-update) | async-done | bytes 1048592 | tf_op jit(solution)/shard_map/all_gather | solution.py:91
  403.7 2.3 copy.60
  (306 shorter events, 136.6 us)
Async XLA Ops:
  6.5 19.4 %copy-start = (bf16[1024,512]{1,0:T(8,128)(2,1)S(1)}, bf16[1024,512]{1,0:T(8,128)(2,1)}, u32[]{:S(2)}) copy-start(bf16[1024,512]{1,0:T(8,128)(2,1)} %param.12) | copy-start | bytes 3145732
  6.5 107.2 %all-gather.5.cloned.1.call-start = ((), (), s32[]{:S(2)}) async-start(), calls=%async_computation | async-start | bytes 1310720 | tf_op jit(solution)/shard_map/all_gather | solution.py:86
  8.5 21.7 %collective-permute-start = (bf16[256,512]{1,0:T(8,128)(2,1)}, bf16[256,512]{1,0:T(8,128)(2,1)S(1)}, u32[]{:S(2)}, u32[]{:S(2)}) collective-permute-start(bf16[256,512]{1,0:T(8,128)(2,1)} %get-tuple-element.250), channel_id=1, source_target_pairs={{0,4},{4,8},{8,12},{12,16},{16,20},{20,24},{24,28},{28,32},{32,36}... | collective-permute-start | bytes 786440 | tf_op jit(solution)/shard_map/ppermute | solution.py:14
  13.3 16.8 %collective-permute-start.1 = (bf16[256,512]{1,0:T(8,128)(2,1)}, bf16[256,512]{1,0:T(8,128)(2,1)}, u32[]{:S(2)}, u32[]{:S(2)}) collective-permute-start(bf16[256,512]{1,0:T(8,128)(2,1)} %get-tuple-element.251), channel_id=1, source_target_pairs={{0,508},{4,0},{8,4},{12,8},{16,12},{20,16},{24,20},{28,24},{32,28}... | collective-permute-start | bytes 786440 | tf_op jit(solution)/shard_map/ppermute | solution.py:14
  84.7 125.6 %all-gather.7.cloned.1.call-start = ((), (), s32[]{:S(2)}) async-start(), calls=%async_computation.1 | async-start | bytes 1310720 | tf_op jit(solution)/shard_map/all_gather | solution.py:91
  113.7 16.2 %copy-start.2 = (bf16[1024,512]{1,0:T(8,128)(2,1)S(1)}, bf16[1024,512]{1,0:T(8,128)(2,1)}, u32[]{:S(2)}) copy-start(bf16[1024,512]{1,0:T(8,128)(2,1)} %all-gather.5.cloned.1.call-done) | copy-start | bytes 3145732
  114.9 13.9 %collective-permute-start.2 = (bf16[256,512]{1,0:T(8,128)(2,1)S(1)}, bf16[256,512]{1,0:T(8,128)(2,1)S(1)}, u32[]{:S(2)}, u32[]{:S(2)}) collective-permute-start(bf16[256,512]{1,0:T(8,128)(2,1)S(1)} %get-tuple-element.248), channel_id=1, source_target_pairs={{0,4},{4,8},{8,12},{12,16},{16,20},{20,24},{24,28},{28,32},{32,36}... | collective-permute-start | bytes 786440 | tf_op jit(solution)/shard_map/ppermute | solution.py:14
  118.1 11.8 %collective-permute-start.3 = (bf16[256,512]{1,0:T(8,128)(2,1)S(1)}, bf16[256,512]{1,0:T(8,128)(2,1)S(1)}, u32[]{:S(2)}, u32[]{:S(2)}) collective-permute-start(bf16[256,512]{1,0:T(8,128)(2,1)S(1)} %get-tuple-element.249), channel_id=1, source_target_pairs={{0,508},{4,0},{8,4},{12,8},{16,12},{20,16},{24,20},{28,24},{32,28}... | collective-permute-start | bytes 786440 | tf_op jit(solution)/shard_map/ppermute | solution.py:14
  180.5 129.3 %all-gather.9.cloned.1.call-start = ((), (), s32[]{:S(2)}) async-start(), calls=%async_computation.2 | async-start | bytes 1310720 | tf_op jit(solution)/shard_map/all_gather | solution.py:86
  211.4 13.9 %collective-permute-start.4 = (bf16[256,512]{1,0:T(8,128)(2,1)S(1)}, bf16[256,512]{1,0:T(8,128)(2,1)S(1)}, u32[]{:S(2)}, u32[]{:S(2)}) collective-permute-start(bf16[256,512]{1,0:T(8,128)(2,1)S(1)} %get-tuple-element.246), channel_id=1, source_target_pairs={{0,4},{4,8},{8,12},{12,16},{16,20},{20,24},{24,28},{28,32},{32,36}... | collective-permute-start | bytes 786440 | tf_op jit(solution)/shard_map/ppermute | solution.py:14
  214.7 11.8 %collective-permute-start.5 = (bf16[256,512]{1,0:T(8,128)(2,1)S(1)}, bf16[256,512]{1,0:T(8,128)(2,1)S(1)}, u32[]{:S(2)}, u32[]{:S(2)}) collective-permute-start(bf16[256,512]{1,0:T(8,128)(2,1)S(1)} %get-tuple-element.247), channel_id=1, source_target_pairs={{0,508},{4,0},{8,4},{12,8},{16,12},{20,16},{24,20},{28,24},{32,28}... | collective-permute-start | bytes 786440 | tf_op jit(solution)/shard_map/ppermute | solution.py:14
  223.2 3.3 copy-start.1
  280.1 123.7 %all-gather.11.cloned.1.call-start = ((), (), s32[]{:S(2)}) async-start(), calls=%async_computation.3 | async-start | bytes 1310720 | tf_op jit(solution)/shard_map/all_gather | solution.py:91
  310.9 13.9 %collective-permute-start.6 = (bf16[256,512]{1,0:T(8,128)(2,1)S(1)}, bf16[256,512]{1,0:T(8,128)(2,1)S(1)}, u32[]{:S(2)}, u32[]{:S(2)}) collective-permute-start(bf16[256,512]{1,0:T(8,128)(2,1)S(1)} %get-tuple-element.244), channel_id=1, source_target_pairs={{0,4},{4,8},{8,12},{12,16},{16,20},{20,24},{24,28},{28,32},{32,36}... | collective-permute-start | bytes 786440 | tf_op jit(solution)/shard_map/ppermute | solution.py:14
  314.2 11.8 %collective-permute-start.7 = (bf16[256,512]{1,0:T(8,128)(2,1)S(1)}, bf16[256,512]{1,0:T(8,128)(2,1)S(1)}, u32[]{:S(2)}, u32[]{:S(2)}) collective-permute-start(bf16[256,512]{1,0:T(8,128)(2,1)S(1)} %get-tuple-element.245), channel_id=1, source_target_pairs={{0,508},{4,0},{8,4},{12,8},{16,12},{20,16},{24,20},{28,24},{32,28}... | collective-permute-start | bytes 786440 | tf_op jit(solution)/shard_map/ppermute | solution.py:14
  373.2 0.7 copy-start.3
Sparse Core Ops, SparseCore 0:
  84.8 28.8 all-gather.4
  180.7 29.6 all-gather.6
  280.2 29.6 all-gather.8
  374.0 29.6 all-gather.10
where the time goes:
time: 415 us; the launch traced here: 413 us
  local copies, waits for them, and re-layouts  132 us (32%)
  waiting for transfers between devices  131 us (32%)
  matrix products  75.4 us (18%)
  starting transfers between devices  40.9 us (10%)
  other arithmetic  18.3 us (4%)
  between operations  13.4 us (3%)
    gather x32, local copies, waits for them, and re-layouts, one_group(): gathered = jnp.take(extended, index_part, axis=0)  64.6 us
    all_gather x2, waiting for transfers between devices, on_device(): current = lax.all_gather(renewed, 'layer', axis=1, tiled=True)  59.6 us
    all_gather x2, waiting for transfers between devices, on_device(): factor = lax.all_gather(factor_part, 'layer', axis=1, tiled=True)  58.7 us
    dot_general x32, matrix products, one_group(): jnp.einsum('rasb,rsbx->rax', left_part, arranged, preferred_element_type=...  53.2 us
    ppermute x8, starting transfers between devices, from_behind(): return lax.ppermute(value, axis, pairs)  40.8 us
    reshape x32, local copies, waits for them, and re-layouts, one_group(): gathered = gathered.reshape(group_rows, slot_count, BS, slot_count, BS)  35.3 us
    dot_general x32, matrix products, one_group(): jnp.einsum('rsbtc,rszt->rsbzc', gathered, select_part, preferred_element_...  22.2 us
    ppermute x8, waiting for transfers between devices, from_behind(): return lax.ppermute(value, axis, pairs)  12.8 us
  transfers between devices with their start and end apart: 12, of which 10 were waited for; matrix products, arithmetic and copies ran while one was open for 3% of the time, Pallas kernels for 0%

commit v1 on v0

v1 whole, which is shorter than its diff:
```python
import jax
import jax.numpy as jnp
from jax import lax
from jax.experimental import pallas as pl
from jax.experimental.pallas import tpu as pltpu
from jax.sharding import PartitionSpec as P

BS = 64
KB = 8
W = 4
SB = W * BS
GROUP = 16
TILE = 128 // GROUP
BUF = 8 * 128
MESH = pl.DeviceIdType.MESH
F32 = jnp.float32
BF16 = jnp.bfloat16


def kernel(
    groups, cols, x_hbm, pat_hbm, out_hbm,
    loc, a_lo, a_hi, b_lo, b_hi, c_lo, c_hi, xd, f0, x1, f1, x2, out_v,
    pat_v, tab_v, tab_s, load_sem, pat_sem, tab_sem, out_sem, send_sem, recv_sem,
):
    row, col, layer = lax.axis_index("row"), lax.axis_index("col"), lax.axis_index("layer")
    me = row * cols + col
    before, after = lax.rem(me + groups - 1, groups), lax.rem(me + 1, groups)

    def device(group):
        return (group // cols, lax.rem(group, cols), layer)

    barrier = pltpu.get_barrier_semaphore()
    for group in (before, after):
        pl.semaphore_signal(barrier, inc=1, device_id=device(group), device_id_type=MESH)

    load = pltpu.make_async_copy(x_hbm, loc.at[:, 0 : KB * BS], load_sem)
    load.start()
    def tile_of(group):
        return pl.ds(pl.multiple_of((group // TILE) * 128, 128), 128)

    pats = [
        pltpu.make_async_copy(pat_hbm.at[:, tile_of(group)], pat_v.at[q], pat_sem.at[q])
        for q, group in enumerate((before, me, after))
    ]
    for copy in pats:
        copy.start()
    for copy in pats:
        copy.wait()

    lane = lax.broadcasted_iota(jnp.int32, (KB, 128), 1)
    slot = lax.broadcasted_iota(jnp.int32, (KB, 128), 0)
    a_of = lane & (W - 1)

    def slot_sum(v):
        for step in (1, 2, 4):
            v = v + pltpu.roll(v, step, 0)
        return v[0:1]

    for q, group in enumerate((before, me, after)):
        off = (pat_v[q] - ((group // TILE) * 128 + lane) + W) & (groups * GROUP - 1)
        for o in range(2 * W + 1):
            code = ((slot ^ (a_of + o)) & 1) * 4 + (slot >> 1) - 8
            tab_v[q, o : o + 1, :] = 8 + slot_sum(jnp.where(off == o, code, 0))
        tab_v[q, 9:10, :] = W * (2 * W + 1) - slot_sum(off)
        if q == 1:
            place = a_of + off
            tab_v[3, 0:KB, :] = ((place ^ slot) & 1) * 6 + (place >> 1)
    table = pltpu.make_async_copy(tab_v, tab_s, tab_sem)
    table.start()
    first_lane = [lax.rem(group, TILE) * GROUP for group in (before, me, after)]

    pl.semaphore_wait(barrier, 2)

    def send(index, src, dst, group):
        return pltpu.make_async_remote_copy(
            src_ref=src, dst_ref=dst, send_sem=send_sem.at[index], recv_sem=recv_sem.at[index],
            device_id=device(group), device_id_type=MESH,
        )

    wide = KB * BS
    copies = {
        ("a", 0): send(0, x_hbm.at[pl.ds(3 * SB, SB)], a_lo.at[:, 0:wide], after),
        ("a", 1): send(1, x_hbm.at[pl.ds(0, SB)], a_hi.at[:, 0:wide], before),
        ("b", 0): send(2, x_hbm.at[pl.ds(2 * SB, SB)], b_lo.at[:, 0:wide], after),
        ("b", 1): send(3, x_hbm.at[pl.ds(SB, SB)], b_hi.at[:, 0:wide], before),
        ("c", 0): send(4, xd.at[pl.ds(3 * SB, SB), 2 * SB : 3 * SB], c_lo, after),
        ("c", 1): send(5, xd.at[pl.ds(4 * SB, SB), 0:SB], c_hi, before),
    }
    for key in (("a", 0), ("a", 1), ("b", 0), ("b", 1)):
        copies[key].start()

    def swap(v):
        return jnp.concatenate([v[:, BS:], v[:, :BS]], axis=1)

    left_half = lax.broadcasted_iota(jnp.int32, (1, 128), 1) < BS

    def pick(planes, first, second):
        number = jnp.where(left_half, first, second).astype(F32).astype(BF16)
        number = jnp.broadcast_to(number, (BS, 128))
        value = jnp.zeros((BS, 128), BF16)
        for index, plane in planes.items():
            value = jnp.where(number == jnp.array(index, BF16), plane, value)
        return value

    def densify(src, src_base, dst_base, q, first):
        rows = pl.ds(src_base, SB)
        for d in range(4):
            src[rows, 512 + 128 * d : 640 + 128 * d] = swap(src[rows, 128 * d : 128 * d + 128])
        for a in range(W):
            rows = pl.ds(src_base + a * BS, BS)
            planes = {d: src[rows, 128 * d : 128 * d + 128] for d in range(8)}
            for d in range(6):
                number = [
                    tab_s[q, o, first_lane[q] + first + a] if 0 <= o <= 2 * W else 8 for o in (2 * d - a, 2 * d + 1 - a)
                ]
                if all(isinstance(n, int) for n in number):
                    value = jnp.zeros((BS, 128), BF16)
                else:
                    value = pick(planes, *number)
                xd[pl.ds(dst_base + a * BS, BS), 128 * d : 128 * d + 128] = value

    load.wait()
    table.wait()

    def local_rows(index, carry):
        densify(loc, index * SB, (index + 2) * SB, 1, index * W)
        return carry

    lax.fori_loop(0, GROUP // W, local_rows, 0)
    copies[("c", 0)].start()
    copies[("c", 1)].start()

    block_lane = lax.broadcasted_iota(jnp.int32, (1, SB), 1) >> 6
    eye = jnp.where(
        lax.broadcasted_iota(jnp.int32, (SB, SB), 0) == lax.broadcasted_iota(jnp.int32, (SB, SB), 1), 1.5, 0.0
    ).astype(F32)

    def block(ref, i, j):
        return ref[(i + 2) * SB : (i + 3) * SB, (j - i + 1) * SB : (j - i + 2) * SB]

    def product(left, right, i, j):
        ks = [k for k in (i - 1, i, i + 1) if abs(k - j) <= 1]
        lo = ks[0] - i + 1
        lhs = left[(i + 2) * SB : (i + 3) * SB, lo * SB : (lo + len(ks)) * SB]
        rhs = []
        for k in ks:
            if right is xd and k == -3:
                rhs.append(c_lo[...])
            elif right is xd and k == 6:
                rhs.append(c_hi[...])
            else:
                rhs.append(block(right, k, j))
        return jnp.dot(lhs, jnp.concatenate(rhs, axis=0), preferred_element_type=F32)

    def masks(i, j):
        out = []
        for a in range(W):
            r = i * W + a
            q, r = (0, r + GROUP) if r < 0 else ((2, r - GROUP) if r >= GROUP else (1, r))
            o = block_lane + ((j - i + 1) * W - a)
            keep = (o != tab_s[q, 9, first_lane[q] + r]) & (o >= 0) & (o <= 2 * W)
            out.append(jnp.where(keep, 1.0, 0.0).astype(F32))
        return out

    def step(dst, left, right, i, j, factor):
        value = product(left, right, i, j)
        keep = masks(i, j)
        pieces = []
        for a in range(W):
            piece = value[a * BS : (a + 1) * BS]
            if factor:
                piece = piece * (keep[a] * -0.5)
                if i == j:
                    piece = piece + eye[a * BS : (a + 1) * BS]
            else:
                piece = piece * keep[a]
            pieces.append(piece.astype(BF16))
        if dst is x2:
            for a in range(W):
                for h in range(2):
                    d = (j - i + 1) * 2 + h
                    part = pieces[a][:, h * 128 : (h + 1) * 128]
                    rows = slice(i * SB + a * BS, i * SB + (a + 1) * BS)
                    x2[rows, d * 128 : d * 128 + 128] = part
                    x2[rows, (d + 6) * 128 : (d + 6) * 128 + 128] = swap(part)
        else:
            for a in range(W):
                top = (i + 2) * SB + a * BS
                dst[top : top + BS, (j - i + 1) * SB : (j - i + 2) * SB] = pieces[a]

    def level(dst, left, right, pairs, factor):
        for i, j in pairs:
            step(dst, left, right, i, j, factor)
            step(dst, left, right, 3 - i, 3 - j, factor)

    def stage(f0_pairs, x1_pairs, f1_pairs, x2_pairs):
        level(f0, xd, xd, f0_pairs, True)
        level(x1, xd, f0, x1_pairs, False)
        level(f1, x1, x1, f1_pairs, True)
        level(x2, x1, f1, x2_pairs, False)

    outs = []

    def finish(i):
        for a in range(W):
            r = i * W + a
            rows = slice(r * BS, (r + 1) * BS)
            chunks = range(a // 2, a // 2 + W + 1)
            planes = {d: x2[rows, 128 * d : 128 * d + 128] for base in (0, 6) for d in (base + c for c in chunks)}
            for d in range(4):
                number = [tab_s[3, s, first_lane[1] + r] for s in (2 * d, 2 * d + 1)]
                out_v[rows, 128 * d : 128 * d + 128] = pick(planes, *number)
        copy = pltpu.make_async_copy(out_v.at[pl.ds(i * SB, SB)], out_hbm.at[pl.ds(i * SB, SB)], out_sem.at[i])
        copy.start()
        outs.append(copy)

    stage([(0, 1), (1, 0), (1, 1), (1, 2)], [(0, 1), (1, 1), (1, 2)], [(1, 2)], [])

    copies[("a", 0)].wait_recv()
    densify(a_lo, 0, SB, 0, 12)
    copies[("a", 1)].wait_recv()
    densify(a_hi, 0, 6 * SB, 2, 0)
    stage([(0, 0), (0, -1), (-1, 0)], [(0, 0), (1, 0), (-1, 0)], [(0, 1), (1, 0), (1, 1)], [(0, 1), (1, 1), (1, 2)])

    copies[("b", 0)].wait_recv()
    densify(b_lo, 0, 0, 0, 8)
    copies[("b", 1)].wait_recv()
    densify(b_hi, 0, 7 * SB, 2, 4)
    stage([(-1, -1), (-1, -2), (-2, -1)], [(0, -1), (-1, -1), (-2, -1)], [(0, 0), (0, -1), (-1, 0)], [(0, 0), (1, 0)])
    finish(1)
    finish(2)

    copies[("c", 0)].wait_recv()
    copies[("c", 1)].wait_recv()
    stage([(-2, -2)], [(-1, -2)], [(-1, -1)], [(0, -1)])
    finish(0)
    finish(3)

    for copy in outs:
        copy.wait()
    for copy in copies.values():
        copy.wait_send()


def solution(mesh):
    groups = mesh.shape["row"] * mesh.shape["col"]
    cols = mesh.shape["col"]

    def on_device(matrix, pattern):
        rows = GROUP * BS

        def body(*refs):
            kernel(groups, cols, *refs)

        any_space = pl.BlockSpec(memory_space=pl.ANY)
        return pl.pallas_call(
            body,
            out_shape=jax.ShapeDtypeStruct((rows, KB * BS), BF16),
            in_specs=[any_space, any_space],
            out_specs=any_space,
            scratch_shapes=[
                pltpu.VMEM((rows, BUF), BF16),
                pltpu.VMEM((SB, BUF), BF16),
                pltpu.VMEM((SB, BUF), BF16),
                pltpu.VMEM((SB, BUF), BF16),
                pltpu.VMEM((SB, BUF), BF16),
                pltpu.VMEM((SB, SB), BF16),
                pltpu.VMEM((SB, SB), BF16),
                pltpu.VMEM((8 * SB, 3 * SB), BF16),
                pltpu.VMEM((8 * SB, 3 * SB), BF16),
                pltpu.VMEM((8 * SB, 3 * SB), BF16),
                pltpu.VMEM((8 * SB, 3 * SB), BF16),
                pltpu.VMEM((rows, 12 * 128), BF16),
                pltpu.VMEM((rows, KB * BS), BF16),
                pltpu.VMEM((3, KB, 128), jnp.int32),
                pltpu.VMEM((4, 16, 128), jnp.int32),
                pltpu.SMEM((4, 16, 128), jnp.int32),
                pltpu.SemaphoreType.DMA,
                pltpu.SemaphoreType.DMA((3,)),
                pltpu.SemaphoreType.DMA,
                pltpu.SemaphoreType.DMA((4,)),
                pltpu.SemaphoreType.DMA((6,)),
                pltpu.SemaphoreType.DMA((6,)),
            ],
            compiler_params=pltpu.CompilerParams(
                collective_id=0, has_side_effects=True, vmem_limit_bytes=62 * 1024 * 1024
            ),
            cost_estimate=pl.CostEstimate(flops=164 * 2 * SB**3, bytes_accessed=8 << 20, transcendentals=0),
        )(matrix, pattern.T)

    return jax.shard_map(
        on_device,
        mesh=mesh,
        in_specs=(P(("row", "col"), None), P()),
        out_specs=P(("row", "col"), None),
        check_vma=False,
    )
```

time: 415 us -> 33.8 us (0.08)
  waiting for transfers between devices: 131 us -> 0 us
  local copies, waits for them, and re-layouts: 132 us -> 2.26 us
  matrix products: 75.4 us -> 0 us
  starting transfers between devices: 40.9 us -> 0 us
  Pallas kernels: 0 us -> 31.3 us
  other arithmetic: 18.3 us -> 0 us
  between operations: 13.4 us -> 0.01 us
    all_gather x4 -> x0, waiting for transfers between devices: 118 us -> none  [the longest x2 59.6 us: on_device(): current = lax.all_gather(renewed, 'layer', axis=1, tiled=True)]
    dot_general x64 -> x0, matrix products: 75.4 us -> none  [the longest x32 53.2 us: one_group(): jnp.einsum('rasb,rsbx->rax', left_part, arranged, preferred_element_type=...]
    gather x33 -> x0, local copies, waits for them, and re-layouts: 65.3 us -> none  [the longest x32 64.6 us: one_group(): gathered = jnp.take(extended, index_part, axis=0)]
    reshape x66 -> x0, local copies, waits for them, and re-layouts: 47.1 us -> none  [the longest x32 35.3 us: one_group(): gathered = gathered.reshape(group_rows, slot_count, BS, slot_count, BS)]
    ppermute x8 -> x0, starting transfers between devices: 40.8 us -> none  [from_behind(): return lax.ppermute(value, axis, pairs)]
    pallas_call x0 -> x1, Pallas kernels: none -> 31.3 us  [on_device(): pl.pallas_call(body, out_shape=jax.ShapeDtypeStruct((rows, KB * BS), BF16...]
    ppermute x8 -> x0, waiting for transfers between devices: 12.8 us -> none  [from_behind(): return lax.ppermute(value, axis, pairs)]
    concatenate x4 -> x0, other arithmetic: 7.13 us -> none  [extend_rows(): stacked = jnp.concatenate([from_before, tile, from_after], axis=0)]
  transfers between devices with their start and end apart: 12 -> 0, of which waited for: 10 -> 0; matrix products, arithmetic and copies ran while one was open for 3% -> 0% of each run, Pallas kernels for 0% -> 0%
where the time goes in v1:
time: 33.8 us; the launch traced here: 33.6 us
  Pallas kernels  31.3 us (93%)
  local copies, waits for them, and re-layouts  2.26 us (7%)
    pallas_call x1, Pallas kernels, on_device(): pl.pallas_call(body, out_shape=jax.ShapeDtypeStruct((rows, KB * BS), BF16...  31.3 us
    unnamed x1, local copies, waits for them, and re-layouts  2.26 us

profile of v1, /device:TPU:1, one launch (start us, length us, event | category | flops | bytes accessed | tf_op | source)
XLA Modules:
  0.0 33.6 jit_solution(17949230639723191847)
XLA Ops:
  0.0 31.3 %shard_map.28 = bf16[1024,512]{1,0:T(8,128)(2,1)} custom-call(bf16[1024,512]{1,0:T(8,128)(2,1)} %refs_0_.1, s32[8,2048]{1,0:T(8,128)} %bitcast.1), custom_call_target="tpu_custom_call" | custom-call | flops 5502926848 | bytes 8388608 | tf_op jit(solution)/shard_map/pallas_call | solution.py:256
  31.3 2.3 %copy.4 = bf16[1024,512]{1,0:T(8,128)(2,1)} copy(bf16[1024,512]{1,0:T(8,128)(2,1)} %shard_map.28) | data formatting | bytes 2097152

commit v2 on v1

--- a/solution.py
+++ b/solution.py
@@ -19,19 +19,27 @@
 
 def kernel(
     groups, cols, x_hbm, pat_hbm, out_hbm,
-    loc, a_lo, a_hi, b_lo, b_hi, c_lo, c_hi, xd, f0, x1, f1, x2, out_v,
-    pat_v, tab_v, tab_s, load_sem, pat_sem, tab_sem, out_sem, send_sem, recv_sem,
+    loc, a_lo, a_hi, xd, f0, x1, f1, x2, out_v,
+    pat_v, tab_v, tab_s, load_sem, pat_sem, tab_sem, out_sem, z_send, z_recv, x_send, x_recv, late,
 ):
     row, col, layer = lax.axis_index("row"), lax.axis_index("col"), lax.axis_index("layer")
     me = row * cols + col
     before, after = lax.rem(me + groups - 1, groups), lax.rem(me + 1, groups)
 
+    first, last = col == 0, col == cols - 1
+    part = lax.rem(layer, 2)
+    partner = (row, col, layer + 1 - 2 * part)
+
     def device(group):
         return (group // cols, lax.rem(group, cols), layer)
 
     barrier = pltpu.get_barrier_semaphore()
-    for group in (before, after):
-        pl.semaphore_signal(barrier, inc=1, device_id=device(group), device_id_type=MESH)
+    pl.semaphore_signal(barrier, inc=1, device_id=device(before), device_id_type=MESH)
+    pl.semaphore_signal(barrier, inc=1, device_id=partner, device_id_type=MESH)
+
+    @pl.when(jnp.logical_not(last))
+    def _():
+        pl.semaphore_signal(barrier, inc=1, device_id=device(after), device_id_type=MESH)
 
     load = pltpu.make_async_copy(x_hbm, loc.at[:, 0 : KB * BS], load_sem)
     load.start()
@@ -69,25 +77,74 @@
     table.start()
     first_lane = [lax.rem(group, TILE) * GROUP for group in (before, me, after)]
 
-    pl.semaphore_wait(barrier, 2)
-
-    def send(index, src, dst, group):
+    @pl.when(first)
+    def _():
+        pl.semaphore_wait(barrier, 2)
+
+    @pl.when(jnp.logical_not(first))
+    def _():
+        pl.semaphore_wait(barrier, 3)
+
+    @pl.when(last)
+    def _():
+        pl.semaphore_signal(late, inc=1, device_id=device(after), device_id_type=MESH)
+
+    def piece(side, index, half, source):
+        def lanes(base, count, step):
+            return pl.ds(pl.multiple_of(base + step * half, 128), count)
+
+        if index < 2:
+            rows = pl.ds((3 * SB if source and side == 0 else 0) + 128 * half + 64 * index, 64)
+            return x_hbm.at[rows] if source else (a_lo, a_hi)[side].at[rows, 0 : KB * BS]
+        if index < 5:
+            base = ((4, 3) if source else (0, 7))[side] * SB
+            left = (2 * SB, 0)[side]
+            if index == 2:
+                return xd.at[pl.ds(base + 128 * half, 128), SB : 2 * SB]
+            if index == 3:
+                return xd.at[pl.ds(base + 128 * half, 128), lanes(left, 128, 128)]
+            return xd.at[pl.ds(base + (128, 0)[side] + 64 * half, 64), pl.ds(left + (0, 128)[side], 128)]
+        base = ((5, 2) if source else (1, 6))[side] * SB
+        left = (0, 2 * SB)[side]
+        if index == 5:
+            return x1.at[pl.ds(base + 128 * half, 128), lanes(left, 128, 128)]
+        return x1.at[pl.ds(base + (0, 128)[side] + 64 * half, 64), pl.ds(left + (128, 0)[side], 128)]
+
+    def over_z(side, index):
         return pltpu.make_async_remote_copy(
-            src_ref=src, dst_ref=dst, send_sem=send_sem.at[index], recv_sem=recv_sem.at[index],
-            device_id=device(group), device_id_type=MESH,
+            src_ref=piece(side, index, part, True), dst_ref=piece(side, index, part, False),
+            send_sem=z_send.at[side, index], recv_sem=z_recv.at[side, index],
+            device_id=device((after, before)[side]), device_id_type=MESH,
         )
 
-    wide = KB * BS
-    copies = {
-        ("a", 0): send(0, x_hbm.at[pl.ds(3 * SB, SB)], a_lo.at[:, 0:wide], after),
-        ("a", 1): send(1, x_hbm.at[pl.ds(0, SB)], a_hi.at[:, 0:wide], before),
-        ("b", 0): send(2, x_hbm.at[pl.ds(2 * SB, SB)], b_lo.at[:, 0:wide], after),
-        ("b", 1): send(3, x_hbm.at[pl.ds(SB, SB)], b_hi.at[:, 0:wide], before),
-        ("c", 0): send(4, xd.at[pl.ds(3 * SB, SB), 2 * SB : 3 * SB], c_lo, after),
-        ("c", 1): send(5, xd.at[pl.ds(4 * SB, SB), 0:SB], c_hi, before),
-    }
-    for key in (("a", 0), ("a", 1), ("b", 0), ("b", 1)):
-        copies[key].start()
+    def over_x(side, index, half):
+        ref = piece(side, index, half, False)
+        return pltpu.make_async_remote_copy(
+            src_ref=ref, dst_ref=ref,
+            send_sem=x_send.at[side, index], recv_sem=x_recv.at[side, index],
+            device_id=partner, device_id_type=MESH,
+        )
+
+    def send(indices):
+        for index in indices:
+            over_z(0, index).start()
+
+        @pl.when(jnp.logical_not(first))
+        def _():
+            for index in indices:
+                over_z(1, index).start()
+
+    def forward(side, indices):
+        for index in indices:
+            over_z(side, index).wait_recv()
+            over_x(side, index, part).start()
+
+    def arrive(side, indices):
+        for index in indices:
+            over_x(side, index, 1 - part).wait_recv()
+
+    SLOTS, NEXT, TRIANGLE = (0, 1), (2, 3, 4), (5, 6)
+    send(SLOTS)
 
     def swap(v):
         return jnp.concatenate([v[:, BS:], v[:, :BS]], axis=1)
@@ -127,8 +184,12 @@
         return carry
 
     lax.fori_loop(0, GROUP // W, local_rows, 0)
-    copies[("c", 0)].start()
-    copies[("c", 1)].start()
+    send(NEXT)
+    blank = jnp.zeros((128, 128), BF16)
+    xd[0:128, 640:768] = blank
+    xd[7 * SB + 128 : 8 * SB, 0:128] = blank
+    x1[SB + 128 : 2 * SB, 0:128] = blank
+    x1[6 * SB : 6 * SB + 128, 640:768] = blank
 
     block_lane = lax.broadcasted_iota(jnp.int32, (1, SB), 1) >> 6
     eye = jnp.where(
@@ -144,12 +205,7 @@
         lhs = left[(i + 2) * SB : (i + 3) * SB, lo * SB : (lo + len(ks)) * SB]
         rhs = []
         for k in ks:
-            if right is xd and k == -3:
-                rhs.append(c_lo[...])
-            elif right is xd and k == 6:
-                rhs.append(c_hi[...])
-            else:
-                rhs.append(block(right, k, j))
+            rhs.append(block(right, k, j))
         return jnp.dot(lhs, jnp.concatenate(rhs, axis=0), preferred_element_type=F32)
 
     def masks(i, j):
@@ -188,16 +244,22 @@
                 top = (i + 2) * SB + a * BS
                 dst[top : top + BS, (j - i + 1) * SB : (j - i + 2) * SB] = pieces[a]
 
-    def level(dst, left, right, pairs, factor):
+    def level(sides, dst, left, right, pairs, factor):
         for i, j in pairs:
-            step(dst, left, right, i, j, factor)
-            step(dst, left, right, 3 - i, 3 - j, factor)
-
-    def stage(f0_pairs, x1_pairs, f1_pairs, x2_pairs):
-        level(f0, xd, xd, f0_pairs, True)
-        level(x1, xd, f0, x1_pairs, False)
-        level(f1, x1, x1, f1_pairs, True)
-        level(x2, x1, f1, x2_pairs, False)
+            for side in sides:
+                step(dst, left, right, *((i, j) if side == 0 else (3 - i, 3 - j)), factor)
+
+    def level_f0(sides, pairs):
+        level(sides, f0, xd, xd, pairs, True)
+
+    def level_x1(sides, pairs):
+        level(sides, x1, xd, f0, pairs, False)
+
+    def level_f1(sides, pairs):
+        level(sides, f1, x1, x1, pairs, True)
+
+    def level_x2(sides, pairs):
+        level(sides, x2, x1, f1, pairs, False)
 
     outs = []
 
@@ -214,32 +276,63 @@
         copy.start()
         outs.append(copy)
 
-    stage([(0, 1), (1, 0), (1, 1), (1, 2)], [(0, 1), (1, 1), (1, 2)], [(1, 2)], [])
-
-    copies[("a", 0)].wait_recv()
-    densify(a_lo, 0, SB, 0, 12)
-    copies[("a", 1)].wait_recv()
-    densify(a_hi, 0, 6 * SB, 2, 0)
-    stage([(0, 0), (0, -1), (-1, 0)], [(0, 0), (1, 0), (-1, 0)], [(0, 1), (1, 0), (1, 1)], [(0, 1), (1, 1), (1, 2)])
-
-    copies[("b", 0)].wait_recv()
-    densify(b_lo, 0, 0, 0, 8)
-    copies[("b", 1)].wait_recv()
-    densify(b_hi, 0, 7 * SB, 2, 4)
-    stage([(-1, -1), (-1, -2), (-2, -1)], [(0, -1), (-1, -1), (-2, -1)], [(0, 0), (0, -1), (-1, 0)], [(0, 0), (1, 0)])
+    both = (0, 1)
+    level_f0(both, [(0, 1), (1, 0), (1, 1), (1, 2)])
+    level_x1(both, [(0, 1), (1, 1), (1, 2)])
+    send(TRIANGLE)
+    level_f1(both, [(1, 2)])
+
+    def near(side):
+        arrive(side, SLOTS)
+        densify((a_lo, a_hi)[side], 0, (SB, 6 * SB)[side], (0, 2)[side], (12, 0)[side])
+        level_f0((side,), [(0, 0), (0, -1), (-1, 0)])
+        level_x1((side,), [(0, 0), (1, 0), (-1, 0)])
+        level_f1((side,), [(0, 1), (1, 0), (1, 1)])
+        level_x2((side,), [(0, 1), (1, 1)])
+
+    def farther(side):
+        arrive(side, NEXT)
+        level_f0((side,), [(-1, -1), (-2, -1)])
+        level_x1((side,), [(0, -1), (-1, -1), (-2, -1)])
+        level_f1((side,), [(0, 0), (0, -1), (-1, 0)])
+        level_x2((side,), [(0, 0), (1, 0)])
+
+    def farthest(side):
+        arrive(side, TRIANGLE)
+        level_f1((side,), [(-1, -1)])
+        level_x2((side,), [(0, -1)])
+
+    forward(1, SLOTS)
+    near(1)
+    forward(1, NEXT)
+    forward(1, TRIANGLE)
+
+    @pl.when(first)
+    def _():
+        pl.semaphore_wait(late, 1)
+        for index in SLOTS + NEXT + TRIANGLE:
+            over_z(1, index).start()
+
+    forward(0, SLOTS)
+    farther(1)
+    farthest(1)
+    finish(3)
+    forward(0, NEXT)
+    near(0)
+    level_x2(both, [(1, 2)])
+    finish(2)
+    forward(0, TRIANGLE)
+    farther(0)
     finish(1)
-    finish(2)
-
-    copies[("c", 0)].wait_recv()
-    copies[("c", 1)].wait_recv()
-    stage([(-2, -2)], [(-1, -2)], [(-1, -1)], [(0, -1)])
+    farthest(0)
     finish(0)
-    finish(3)
 
     for copy in outs:
         copy.wait()
-    for copy in copies.values():
-        copy.wait_send()
+    for side in both:
+        for index in SLOTS + NEXT + TRIANGLE:
+            over_z(side, index).wait_send()
+            over_x(side, index, part).wait_send()
 
 
 def solution(mesh):
@@ -262,10 +355,6 @@
                 pltpu.VMEM((rows, BUF), BF16),
                 pltpu.VMEM((SB, BUF), BF16),
                 pltpu.VMEM((SB, BUF), BF16),
-                pltpu.VMEM((SB, BUF), BF16),
-                pltpu.VMEM((SB, BUF), BF16),
-                pltpu.VMEM((SB, SB), BF16),
-                pltpu.VMEM((SB, SB), BF16),
                 pltpu.VMEM((8 * SB, 3 * SB), BF16),
                 pltpu.VMEM((8 * SB, 3 * SB), BF16),
                 pltpu.VMEM((8 * SB, 3 * SB), BF16),
@@ -279,13 +368,16 @@
                 pltpu.SemaphoreType.DMA((3,)),
                 pltpu.SemaphoreType.DMA,
                 pltpu.SemaphoreType.DMA((4,)),
-                pltpu.SemaphoreType.DMA((6,)),
-                pltpu.SemaphoreType.DMA((6,)),
+                pltpu.SemaphoreType.DMA((2, 7)),
+                pltpu.SemaphoreType.DMA((2, 7)),
+                pltpu.SemaphoreType.DMA((2, 7)),
+                pltpu.SemaphoreType.DMA((2, 7)),
+                pltpu.SemaphoreType.REGULAR,
             ],
             compiler_params=pltpu.CompilerParams(
                 collective_id=0, has_side_effects=True, vmem_limit_bytes=62 * 1024 * 1024
             ),
-            cost_estimate=pl.CostEstimate(flops=164 * 2 * SB**3, bytes_accessed=8 << 20, transcendentals=0),
+            cost_estimate=pl.CostEstimate(flops=150 * 2 * SB**3, bytes_accessed=8 << 20, transcendentals=0),
         )(matrix, pattern.T)
 
     return jax.shard_map(

time: 33.8 us -> 35.3 us (1.044)
  the two profiles are of different devices: /device:TPU:1 before, /device:TPU:475 now
where the time goes in v2:
time: 35.3 us; the launch traced here: 35.1 us
  Pallas kernels  32.9 us (93%)
  local copies, waits for them, and re-layouts  2.26 us (6%)
    pallas_call x1, Pallas kernels, on_device(): pl.pallas_call(body, out_shape=jax.ShapeDtypeStruct((rows, KB * BS), BF16...  32.9 us
    unnamed x1, local copies, waits for them, and re-layouts  2.26 us

profile of v2, /device:TPU:475, one launch (start us, length us, event | category | flops | bytes accessed | tf_op | source)
XLA Modules:
  0.0 35.1 jit_solution(12892015696328460790)
XLA Ops:
  0.0 32.9 %shard_map.28 = bf16[1024,512]{1,0:T(8,128)(2,1)} custom-call(bf16[1024,512]{1,0:T(8,128)(2,1)} %refs_0_.1, s32[8,2048]{1,0:T(8,128)} %bitcast.1), custom_call_target="tpu_custom_call" | custom-call | flops 5033164800 | bytes 8388608 | tf_op jit(solution)/shard_map/pallas_call | solution.py:349
  32.9 2.3 %copy.4 = bf16[1024,512]{1,0:T(8,128)(2,1)} copy(bf16[1024,512]{1,0:T(8,128)(2,1)} %shard_map.28) | data formatting | bytes 2097152

commit v3 on v2

--- a/solution.py
+++ b/solution.py
@@ -20,7 +20,7 @@
 def kernel(
     groups, cols, x_hbm, pat_hbm, out_hbm,
     loc, a_lo, a_hi, xd, f0, x1, f1, x2, out_v,
-    pat_v, tab_v, tab_s, load_sem, pat_sem, tab_sem, out_sem, z_send, z_recv, x_send, x_recv, late,
+    pat_v, tab_v, tab_s, load_sem, pat_sem, tab_sem, out_sem, z_send, z_recv, x_send, late, late_x,
 ):
     row, col, layer = lax.axis_index("row"), lax.axis_index("col"), lax.axis_index("layer")
     me = row * cols + col
@@ -33,9 +33,14 @@
     def device(group):
         return (group // cols, lax.rem(group, cols), layer)
 
+    edge = jnp.logical_or(first, last)
+    edge_even, edge_odd = jnp.logical_and(edge, part == 0), jnp.logical_and(edge, part == 1)
     barrier = pltpu.get_barrier_semaphore()
     pl.semaphore_signal(barrier, inc=1, device_id=device(before), device_id_type=MESH)
-    pl.semaphore_signal(barrier, inc=1, device_id=partner, device_id_type=MESH)
+
+    @pl.when(edge_even)
+    def _():
+        pl.semaphore_signal(barrier, inc=1, device_id=partner, device_id_type=MESH)
 
     @pl.when(jnp.logical_not(last))
     def _():
@@ -52,38 +57,11 @@
     ]
     for copy in pats:
         copy.start()
-    for copy in pats:
-        copy.wait()
-
-    lane = lax.broadcasted_iota(jnp.int32, (KB, 128), 1)
-    slot = lax.broadcasted_iota(jnp.int32, (KB, 128), 0)
-    a_of = lane & (W - 1)
-
-    def slot_sum(v):
-        for step in (1, 2, 4):
-            v = v + pltpu.roll(v, step, 0)
-        return v[0:1]
-
-    for q, group in enumerate((before, me, after)):
-        off = (pat_v[q] - ((group // TILE) * 128 + lane) + W) & (groups * GROUP - 1)
-        for o in range(2 * W + 1):
-            code = ((slot ^ (a_of + o)) & 1) * 4 + (slot >> 1) - 8
-            tab_v[q, o : o + 1, :] = 8 + slot_sum(jnp.where(off == o, code, 0))
-        tab_v[q, 9:10, :] = W * (2 * W + 1) - slot_sum(off)
-        if q == 1:
-            place = a_of + off
-            tab_v[3, 0:KB, :] = ((place ^ slot) & 1) * 6 + (place >> 1)
-    table = pltpu.make_async_copy(tab_v, tab_s, tab_sem)
-    table.start()
-    first_lane = [lax.rem(group, TILE) * GROUP for group in (before, me, after)]
-
-    @pl.when(first)
-    def _():
-        pl.semaphore_wait(barrier, 2)
-
-    @pl.when(jnp.logical_not(first))
-    def _():
-        pl.semaphore_wait(barrier, 3)
+    pl.semaphore_wait(barrier, 2 - jnp.where(first, 1, 0) + jnp.where(edge_odd, 1, 0))
+
+    @pl.when(edge_odd)
+    def _():
+        pl.semaphore_signal(late_x, inc=1, device_id=partner, device_id_type=MESH)
 
     @pl.when(last)
     def _():
@@ -110,41 +88,85 @@
             return x1.at[pl.ds(base + 128 * half, 128), lanes(left, 128, 128)]
         return x1.at[pl.ds(base + (0, 128)[side] + 64 * half, 64), pl.ds(left + (128, 0)[side], 128)]
 
-    def over_z(side, index):
+    def over_z(side, index, half):
+        mine = jnp.where(half == part, 0, 1)
         return pltpu.make_async_remote_copy(
-            src_ref=piece(side, index, part, True), dst_ref=piece(side, index, part, False),
-            send_sem=z_send.at[side, index], recv_sem=z_recv.at[side, index],
+            src_ref=piece(side, index, half, True), dst_ref=piece(side, index, half, False),
+            send_sem=z_send.at[side, index, mine], recv_sem=z_recv.at[side, index, mine],
             device_id=device((after, before)[side]), device_id_type=MESH,
         )
 
-    def over_x(side, index, half):
-        ref = piece(side, index, half, False)
+    def over_x(side, index):
+        ref = piece(side, index, part, False)
         return pltpu.make_async_remote_copy(
-            src_ref=ref, dst_ref=ref,
-            send_sem=x_send.at[side, index], recv_sem=x_recv.at[side, index],
+            src_ref=ref, dst_ref=ref, send_sem=x_send.at[index], recv_sem=z_recv.at[side, index, 1],
             device_id=partner, device_id_type=MESH,
         )
 
+    def send_before(indices):
+        for index in indices:
+            over_z(1, index, part).start()
+
+            @pl.when(jnp.logical_not(first))
+            def _():
+                over_z(1, index, 1 - part).start()
+
     def send(indices):
         for index in indices:
-            over_z(0, index).start()
+            over_z(0, index, part).start()
+
+            @pl.when(jnp.logical_not(last))
+            def _():
+                over_z(0, index, 1 - part).start()
 
         @pl.when(jnp.logical_not(first))
         def _():
+            send_before(indices)
+
+    forwards = (first, last)
+
+    def forward(side, indices):
+        @pl.when(forwards[side])
+        def _():
             for index in indices:
-                over_z(1, index).start()
-
-    def forward(side, indices):
-        for index in indices:
-            over_z(side, index).wait_recv()
-            over_x(side, index, part).start()
+                over_z(side, index, part).wait_recv()
+                over_x(side, index).start()
 
     def arrive(side, indices):
         for index in indices:
-            over_x(side, index, 1 - part).wait_recv()
+            @pl.when(jnp.logical_not(forwards[side]))
+            def _():
+                over_z(side, index, part).wait_recv()
+
+            over_z(side, index, 1 - part).wait_recv()
 
     SLOTS, NEXT, TRIANGLE = (0, 1), (2, 3, 4), (5, 6)
     send(SLOTS)
+
+    for copy in pats:
+        copy.wait()
+
+    lane = lax.broadcasted_iota(jnp.int32, (KB, 128), 1)
+    slot = lax.broadcasted_iota(jnp.int32, (KB, 128), 0)
+    a_of = lane & (W - 1)
+
+    def slot_sum(v):
+        for step in (1, 2, 4):
+            v = v + pltpu.roll(v, step, 0)
+        return v[0:1]
+
+    for q, group in enumerate((before, me, after)):
+        off = (pat_v[q] - ((group // TILE) * 128 + lane) + W) & (groups * GROUP - 1)
+        for o in range(2 * W + 1):
+            code = ((slot ^ (a_of + o)) & 1) * 4 + (slot >> 1) - 8
+            tab_v[q, o : o + 1, :] = 8 + slot_sum(jnp.where(off == o, code, 0))
+        tab_v[q, 9:10, :] = W * (2 * W + 1) - slot_sum(off)
+        if q == 1:
+            place = a_of + off
+            tab_v[3, 0:KB, :] = ((place ^ slot) & 1) * 6 + (place >> 1)
+    table = pltpu.make_async_copy(tab_v, tab_s, tab_sem)
+    table.start()
+    first_lane = [lax.rem(group, TILE) * GROUP for group in (before, me, after)]
 
     def swap(v):
         return jnp.concatenate([v[:, BS:], v[:, :BS]], axis=1)
@@ -302,37 +324,51 @@
         level_f1((side,), [(-1, -1)])
         level_x2((side,), [(0, -1)])
 
+    @pl.when(edge_even)
+    def _():
+        pl.semaphore_wait(late_x, 1)
+
+    @pl.when(first)
+    def _():
+        pl.semaphore_wait(late, 1)
+        send_before(SLOTS + NEXT + TRIANGLE)
+
     forward(1, SLOTS)
     near(1)
     forward(1, NEXT)
-    forward(1, TRIANGLE)
-
-    @pl.when(first)
-    def _():
-        pl.semaphore_wait(late, 1)
-        for index in SLOTS + NEXT + TRIANGLE:
-            over_z(1, index).start()
-
     forward(0, SLOTS)
-    farther(1)
-    farthest(1)
-    finish(3)
     forward(0, NEXT)
     near(0)
     level_x2(both, [(1, 2)])
+    forward(1, TRIANGLE)
+    forward(0, TRIANGLE)
+    farther(1)
     finish(2)
-    forward(0, TRIANGLE)
     farther(0)
     finish(1)
+    farthest(1)
+    finish(3)
     farthest(0)
     finish(0)
 
     for copy in outs:
         copy.wait()
-    for side in both:
-        for index in SLOTS + NEXT + TRIANGLE:
-            over_z(side, index).wait_send()
-            over_x(side, index, part).wait_send()
+    for index in SLOTS + NEXT + TRIANGLE:
+        over_z(0, index, part).wait_send()
+        over_z(1, index, part).wait_send()
+
+        @pl.when(jnp.logical_not(last))
+        def _():
+            over_z(0, index, 1 - part).wait_send()
+
+        @pl.when(jnp.logical_not(first))
+        def _():
+            over_z(1, index, 1 - part).wait_send()
+
+        for side in both:
+            @pl.when(forwards[side])
+            def _():
+                over_x(side, index).wait_send()
 
 
 def solution(mesh):
@@ -368,10 +404,10 @@
                 pltpu.SemaphoreType.DMA((3,)),
                 pltpu.SemaphoreType.DMA,
                 pltpu.SemaphoreType.DMA((4,)),
-                pltpu.SemaphoreType.DMA((2, 7)),
-                pltpu.SemaphoreType.DMA((2, 7)),
-                pltpu.SemaphoreType.DMA((2, 7)),
-                pltpu.SemaphoreType.DMA((2, 7)),
+                pltpu.SemaphoreType.DMA((2, 7, 2)),
+                pltpu.SemaphoreType.DMA((2, 7, 2)),
+                pltpu.SemaphoreType.DMA((7,)),
+                pltpu.SemaphoreType.REGULAR,
                 pltpu.SemaphoreType.REGULAR,
             ],
             compiler_params=pltpu.CompilerParams(

time: 35.3 us -> 30.7 us (0.87)
  the two profiles are of different devices: /device:TPU:475 before, /device:TPU:2 now
where the time goes in v3:
time: 30.7 us; the launch traced here: 30.5 us
  Pallas kernels  28.2 us (92%)
  local copies, waits for them, and re-layouts  2.26 us (7%)
    pallas_call x1, Pallas kernels, on_device(): pl.pallas_call(body, out_shape=jax.ShapeDtypeStruct((rows, KB * BS), BF16...  28.2 us
    unnamed x1, local copies, waits for them, and re-layouts  2.26 us

profile of v3, /device:TPU:2, one launch (start us, length us, event | category | flops | bytes accessed | tf_op | source)
XLA Modules:
  0.0 30.5 jit_solution(16069033730657964371)
XLA Ops:
  0.0 28.2 %shard_map.28 = bf16[1024,512]{1,0:T(8,128)(2,1)} custom-call(bf16[1024,512]{1,0:T(8,128)(2,1)} %refs_0_.1, s32[8,2048]{1,0:T(8,128)} %bitcast.1), custom_call_target="tpu_custom_call" | custom-call | flops 5033164800 | bytes 8388608 | tf_op jit(solution)/shard_map/pallas_call | solution.py:385
  28.2 2.3 %copy.4 = bf16[1024,512]{1,0:T(8,128)(2,1)} copy(bf16[1024,512]{1,0:T(8,128)(2,1)} %shard_map.28) | data formatting | bytes 2097152

commit v4 on v3

--- a/solution.py
+++ b/solution.py
@@ -337,12 +337,21 @@
     near(1)
     forward(1, NEXT)
     forward(0, SLOTS)
+
+    @pl.when(first)
+    def _():
+        farther(1)
+
     forward(0, NEXT)
     near(0)
-    level_x2(both, [(1, 2)])
     forward(1, TRIANGLE)
     forward(0, TRIANGLE)
-    farther(1)
+    level_x2(both, [(1, 2)])
+
+    @pl.when(jnp.logical_not(first))
+    def _():
+        farther(1)
+
     finish(2)
     farther(0)
     finish(1)
@@ -384,7 +393,7 @@
         any_space = pl.BlockSpec(memory_space=pl.ANY)
         return pl.pallas_call(
             body,
-            out_shape=jax.ShapeDtypeStruct((rows, KB * BS), BF16),
+            out_shape=pltpu.VMEM((rows, KB * BS), BF16),
             in_specs=[any_space, any_space],
             out_specs=any_space,
             scratch_shapes=[
@@ -411,7 +420,7 @@
                 pltpu.SemaphoreType.REGULAR,
             ],
             compiler_params=pltpu.CompilerParams(
-                collective_id=0, has_side_effects=True, vmem_limit_bytes=62 * 1024 * 1024
+                collective_id=0, has_side_effects=True, vmem_limit_bytes=56 * 1024 * 1024
             ),
             cost_estimate=pl.CostEstimate(flops=150 * 2 * SB**3, bytes_accessed=8 << 20, transcendentals=0),
         )(matrix, pattern.T)

time: 30.7 us -> 28.2 us (0.919)
  the two profiles are of different devices: /device:TPU:2 before, /device:TPU:60 now
where the time goes in v4:
time: 28.2 us; the launch traced here: 28.1 us
  Pallas kernels  27.1 us (96%)
  local copies, waits for them, and re-layouts  0.97 us (3%)
    pallas_call x1, Pallas kernels, on_device(): pl.pallas_call(body, out_shape=pltpu.VMEM((rows, KB * BS), BF16), in_spec...  27.1 us
    unnamed x1, local copies, waits for them, and re-layouts  0.97 us

profile of v4, /device:TPU:60, one launch (start us, length us, event | category | flops | bytes accessed | tf_op | source)
XLA Modules:
  0.0 28.1 jit_solution(2071371938581867791)
XLA Ops:
  0.0 27.1 %shard_map.28 = bf16[1024,512]{1,0:T(8,128)(2,1)S(1)} custom-call(bf16[1024,512]{1,0:T(8,128)(2,1)} %refs_0_.1, s32[8,2048]{1,0:T(8,128)} %bitcast.1), custom_call_target="tpu_custom_call" | custom-call | flops 5033164800 | bytes 8388608 | tf_op jit(solution)/shard_map/pallas_call | solution.py:394
  27.1 1.0 %copy.4 = bf16[1024,512]{1,0:T(8,128)(2,1)} copy(bf16[1024,512]{1,0:T(8,128)(2,1)S(1)} %shard_map.28) | data formatting | bytes 2097152

commit v5 on v4

--- a/solution.py
+++ b/solution.py
@@ -18,9 +18,9 @@
 
 
 def kernel(
-    groups, cols, x_hbm, pat_hbm, out_hbm,
-    loc, a_lo, a_hi, xd, f0, x1, f1, x2, out_v,
-    pat_v, tab_v, tab_s, load_sem, pat_sem, tab_sem, out_sem, z_send, z_recv, x_send, late, late_x,
+    groups, cols, x_hbm, pat_hbm, out_v,
+    loc, a_lo, a_hi, xd, f0, x1, f1, x2,
+    pat_v, tab_v, tab_s, load_sem, pat_sem, tab_sem, z_send, z_recv, x_send, late, late_x,
 ):
     row, col, layer = lax.axis_index("row"), lax.axis_index("col"), lax.axis_index("layer")
     me = row * cols + col
@@ -283,8 +283,6 @@
     def level_x2(sides, pairs):
         level(sides, x2, x1, f1, pairs, False)
 
-    outs = []
-
     def finish(i):
         for a in range(W):
             r = i * W + a
@@ -294,9 +292,6 @@
             for d in range(4):
                 number = [tab_s[3, s, first_lane[1] + r] for s in (2 * d, 2 * d + 1)]
                 out_v[rows, 128 * d : 128 * d + 128] = pick(planes, *number)
-        copy = pltpu.make_async_copy(out_v.at[pl.ds(i * SB, SB)], out_hbm.at[pl.ds(i * SB, SB)], out_sem.at[i])
-        copy.start()
-        outs.append(copy)
 
     both = (0, 1)
     level_f0(both, [(0, 1), (1, 0), (1, 1), (1, 2)])
@@ -337,15 +332,15 @@
     near(1)
     forward(1, NEXT)
     forward(0, SLOTS)
+    forward(0, NEXT)
 
     @pl.when(first)
     def _():
         farther(1)
 
-    forward(0, NEXT)
+    forward(0, TRIANGLE)
     near(0)
     forward(1, TRIANGLE)
-    forward(0, TRIANGLE)
     level_x2(both, [(1, 2)])
 
     @pl.when(jnp.logical_not(first))
@@ -353,15 +348,13 @@
         farther(1)
 
     finish(2)
-    farther(0)
-    finish(1)
     farthest(1)
     finish(3)
+    farther(0)
     farthest(0)
+    finish(1)
     finish(0)
 
-    for copy in outs:
-        copy.wait()
     for index in SLOTS + NEXT + TRIANGLE:
         over_z(0, index, part).wait_send()
         over_z(1, index, part).wait_send()
@@ -395,7 +388,7 @@
             body,
             out_shape=pltpu.VMEM((rows, KB * BS), BF16),
             in_specs=[any_space, any_space],
-            out_specs=any_space,
+            out_specs=pl.BlockSpec(memory_space=pltpu.VMEM),
             scratch_shapes=[
                 pltpu.VMEM((rows, BUF), BF16),
                 pltpu.VMEM((SB, BUF), BF16),
@@ -405,14 +398,12 @@
                 pltpu.VMEM((8 * SB, 3 * SB), BF16),
                 pltpu.VMEM((8 * SB, 3 * SB), BF16),
                 pltpu.VMEM((rows, 12 * 128), BF16),
-                pltpu.VMEM((rows, KB * BS), BF16),
                 pltpu.VMEM((3, KB, 128), jnp.int32),
                 pltpu.VMEM((4, 16, 128), jnp.int32),
                 pltpu.SMEM((4, 16, 128), jnp.int32),
                 pltpu.SemaphoreType.DMA,
                 pltpu.SemaphoreType.DMA((3,)),
                 pltpu.SemaphoreType.DMA,
-                pltpu.SemaphoreType.DMA((4,)),
                 pltpu.SemaphoreType.DMA((2, 7, 2)),
                 pltpu.SemaphoreType.DMA((2, 7, 2)),
                 pltpu.SemaphoreType.DMA((7,)),

time: 28.2 us -> 28 us (level)
  the two profiles are of different devices: /device:TPU:60 before, /device:TPU:2 now
where the time goes in v5:
time: 28 us; the launch traced here: 27.9 us
  Pallas kernels  26.9 us (96%)
  local copies, waits for them, and re-layouts  0.97 us (3%)
    pallas_call x1, Pallas kernels, on_device(): pl.pallas_call(body, out_shape=pltpu.VMEM((rows, KB * BS), BF16), in_spec...  26.9 us
    unnamed x1, local copies, waits for them, and re-layouts  0.97 us

profile of v5, /device:TPU:2, one launch (start us, length us, event | category | flops | bytes accessed | tf_op | source)
XLA Modules:
  0.0 27.9 jit_solution(12968740070619281561)
XLA Ops:
  0.0 26.9 %shard_map.28 = bf16[1024,512]{1,0:T(8,128)(2,1)S(1)} custom-call(bf16[1024,512]{1,0:T(8,128)(2,1)} %refs_0_.1, s32[8,2048]{1,0:T(8,128)} %bitcast.1), custom_call_target="tpu_custom_call" | custom-call | flops 5033164800 | bytes 8388608 | tf_op jit(solution)/shard_map/pallas_call | solution.py:387
  26.9 1.0 %copy.4 = bf16[1024,512]{1,0:T(8,128)(2,1)} copy(bf16[1024,512]{1,0:T(8,128)(2,1)S(1)} %shard_map.28) | data formatting | bytes 2097152
